TPU v7x, 32 devices: a whole 2x2x4 slice. The times are simulated.
32 devices in a mesh: layer: 2 (over core), row: 16 (over z, y, x).
Axes of the slice: x: 2, y: 2, z: 4, core: 2. Of those that a mesh axis runs over, the one named last changes fastest.
Arguments:
- residual: float32 [2, 2, 16, 1024, 192], P(None, None, 'layer', 'row'), may hold values from -6 to 6
- wavenumber: float32 [16, 1024, 192], P('layer', 'row'), may hold values from 0.25 to 1.5
- inverse: bfloat16 [2, 2, 3072, 3072], P(None, 'layer', 'row'), may hold values from -3 to 3
Outputs:
- preconditioned: float32 [2, 2, 16, 1024, 192], P(None, None, 'layer', 'row')
All inputs are finite; a program needn't handle non-finite values.
Results may differ from a plain program's by a relative error of at most 0.003.
Values may be sent and summed in bfloat16 or wider, within the bound.
A program may use at most 64 MiB of HBM per device.

v0:
```python
import jax
import jax.numpy as jnp
from jax import lax
from jax.sharding import PartitionSpec as P

QY = 16
PX = 4
SWEEPS = 4


damping = 0.8
absorb = 0.5
coupling = 0.45


def extended_2(block, sides, width):
    for axis, dim in sides:
        count = lax.axis_size(axis)
        forward = [(i, i + 1) for i in range(count - 1)]
        backward = [(target, source) for source, target in forward]
        low = lax.ppermute(
            lax.slice_in_dim(block, block.shape[dim] - width, None, axis=dim), axis, forward
        )
        high = lax.ppermute(lax.slice_in_dim(block, 0, width, axis=dim), axis, backward)
        block = jnp.concatenate([low, block, high], axis=dim)
    return block


def from_behind(block, axis, distance):
    devices = range(lax.axis_size(axis))
    route = [(i - distance, i) for i in devices if i - distance in devices]
    return lax.ppermute(block, axis, route)


def diagonal_parts(wavenumber):
    real_part = 6.0 - wavenumber
    imag_part = -absorb * wavenumber
    modulus = real_part * real_part + imag_part * imag_part
    return (real_part, imag_part, real_part / modulus, -imag_part / modulus)


def first_sweep(source, reciprocal_re, reciprocal_im):
    update_re = reciprocal_re * source[:, 0] - reciprocal_im * source[:, 1]
    update_im = reciprocal_re * source[:, 1] + reciprocal_im * source[:, 0]
    return damping * jnp.stack([update_re, update_im], axis=1)


def relax(extended, source, diagonal_re, diagonal_im, reciprocal_re, reciprocal_im):
    centre = extended[:, :, 1:-1, 1:-1, :]
    beside = extended[:, :, 2:, 1:-1, :] + extended[:, :, :-2, 1:-1, :]
    beside = beside + extended[:, :, 1:-1, 2:, :] + extended[:, :, 1:-1, :-2, :]
    padded = jnp.pad(centre, ((0, 0), (0, 0), (0, 0), (0, 0), (1, 1)))
    beside = beside + padded[..., 2:] + padded[..., :-2]
    applied_re = diagonal_re * centre[:, 0] - diagonal_im * centre[:, 1] - beside[:, 0]
    applied_im = diagonal_re * centre[:, 1] + diagonal_im * centre[:, 0] - beside[:, 1]
    remain_re = source[:, 0] - applied_re
    remain_im = source[:, 1] - applied_im
    update_re = reciprocal_re * remain_re - reciprocal_im * remain_im
    update_im = reciprocal_re * remain_im + reciprocal_im * remain_re
    return centre + damping * jnp.stack([update_re, update_im], axis=1)


def on_device(residual, wavenumber, inverse):
    shot_count = residual.shape[0]
    slab_depth = residual.shape[2]
    height = residual.shape[3]
    across = residual.shape[4]
    diagonal_re, diagonal_im, reciprocal_re, reciprocal_im = diagonal_parts(wavenumber)
    iterate = first_sweep(residual, reciprocal_re, reciprocal_im)
    for counter in range(SWEEPS - 1):
        extended = extended_2(iterate.astype(jnp.bfloat16), (("layer", 2), ("row", 3)), 1).astype(
            iterate.dtype
        )
        iterate = relax(extended, residual, diagonal_re, diagonal_im, reciprocal_re, reciprocal_im)
    blocks = residual.reshape(shot_count, 2, slab_depth, height // QY, QY, across // PX, PX).mean(
        axis=(2, 4, 6)
    )
    coarse_rhs = blocks.reshape(shot_count, 2, -1).transpose(1, 0, 2)
    matrix_re = inverse[0, 0]
    matrix_im = inverse[1, 0]
    layers = lax.axis_size("layer")

    def fold_into(shard_piece):
        product_re = jnp.einsum(
            "rc,ksc->ksr", matrix_re, shard_piece, preferred_element_type=jnp.float32
        )
        product_im = jnp.einsum(
            "rc,ksc->ksr", matrix_im, shard_piece, preferred_element_type=jnp.float32
        )
        return jnp.stack([product_re[0] - product_im[1], product_re[1] + product_im[0]])

    def advance_all(counter, solved):
        incoming = from_behind(solved, "layer", 1)
        vector = (coarse_rhs + coupling * incoming).astype(jnp.bfloat16)
        return fold_into(lax.all_gather(vector, "row", axis=2, tiled=True))

    coarse = lax.fori_loop(0, layers, advance_all, jnp.zeros_like(coarse_rhs))
    lifted = coarse.transpose(1, 0, 2).reshape(shot_count, 2, 1, height // QY, 1, across // PX, 1)
    lifted = jnp.broadcast_to(
        lifted, (shot_count, 2, slab_depth, height // QY, QY, across // PX, PX)
    )
    lifted = lifted.reshape(shot_count, 2, slab_depth, height, across)
    return iterate + lifted


def solution(mesh):
    return jax.shard_map(
        on_device,
        mesh=mesh,
        in_specs=(
            P(None, None, "layer", "row", None),
            P("layer", "row", None),
            P(None, "layer", "row", None),
        ),
        out_specs=P(None, None, "layer", "row", None),
        check_vma=False,
    )
```

profile of v0, /device:TPU:0, one launch (start us, length us, event | category | flops | bytes accessed | tf_op | source)
XLA Modules:
  0.0 182.6 jit_solution(16802226898958387212)
XLA Ops:
  0.0 1.4 broadcast_subtract_fusion
  2.4 2.4 %collective-permute-start.1 = (bf16[2,2,1,64,192]{4,3,2,1,0:T(8,128)(2,1)S(1)}, bf16[2,2,1,64,192]{4,3,2,1,0:T(8,128)(2,1)S(1)}, u32[]{:S(2)}, u32[]{:S(2)}) collective-permute-start(bf16[2,2,1,64,192]{4,3,2,1,0:T(8,128)(2,1)S(1)} %get-tuple-element.78), channel_id=1, source_target_pairs={{0,16},{1,17},{2,18},{3,19},{4,20},{5,21},{6,22},{7,23},{8,24},{9,... | collective-permute-start | bytes 294920 | tf_op jit(solution)/shard_map/ppermute | solution.py:21
  4.8 1.3 collective-permute-start.2
  6.1 1.9 %collective-permute-done.2 = bf16[2,2,1,64,192]{4,3,2,1,0:T(8,128)(2,1)S(1)} collective-permute-done((bf16[2,2,1,64,192]{4,3,2,1,0:T(8,128)(2,1)S(1)}, bf16[2,2,1,64,192]{4,3,2,1,0:T(8,128)(2,1)S(1)}, u32[]{:S(2)}, u32[]{:S(2)}) %collective-permute-start.2) | collective-permute-done | bytes 98336 | tf_op jit(solution)/shard_map/ppermute | solution.py:24
  8.1 4.2 %collective-permute-start.3 = (bf16[2,2,10,1,192]{4,3,2,1,0:T(2,128)(2,1)S(1)}, bf16[2,2,10,1,192]{4,3,2,1,0:T(2,128)(2,1)S(1)}, u32[]{:S(2)}, u32[]{:S(2)}) collective-permute-start(bf16[2,2,10,1,192]{4,3,2,1,0:T(2,128)(2,1)S(1)} %get-tuple-element.72), channel_id=1, source_target_pairs={{0,1},{1,2},{2,3},{3,4},{4,5},{5,6},{6,7},{7,8},{8,9},{9,10},{10,1... | collective-permute-start | bytes 46088 | tf_op jit(solution)/shard_map/ppermute | solution.py:21
  12.3 1.3 collective-permute-start.4
  14.0 4.2 %collective-permute-done.4 = bf16[2,2,10,1,192]{4,3,2,1,0:T(2,128)(2,1)S(1)} collective-permute-done((bf16[2,2,10,1,192]{4,3,2,1,0:T(2,128)(2,1)S(1)}, bf16[2,2,10,1,192]{4,3,2,1,0:T(2,128)(2,1)S(1)}, u32[]{:S(2)}, u32[]{:S(2)}) %collective-permute-start.4) | collective-permute-done | bytes 15392 | tf_op jit(solution)/shard_map/ppermute | solution.py:24
  22.0 1.4 collective-permute-start.5
  23.4 1.3 collective-permute-start.6
  24.7 1.9 %collective-permute-done.6 = bf16[2,2,1,64,192]{4,3,2,1,0:T(8,128)(2,1)S(1)} collective-permute-done((bf16[2,2,1,64,192]{4,3,2,1,0:T(8,128)(2,1)S(1)}, bf16[2,2,1,64,192]{4,3,2,1,0:T(8,128)(2,1)S(1)}, u32[]{:S(2)}, u32[]{:S(2)}) %collective-permute-start.6) | collective-permute-done | bytes 98336 | tf_op jit(solution)/shard_map/ppermute | solution.py:24
  27.4 4.9 %collective-permute-start.7 = (bf16[2,2,10,1,192]{4,3,2,1,0:T(2,128)(2,1)}, bf16[2,2,10,1,192]{4,3,2,1,0:T(2,128)(2,1)}, u32[]{:S(2)}, u32[]{:S(2)}) collective-permute-start(bf16[2,2,10,1,192]{4,3,2,1,0:T(2,128)(2,1)} %get-tuple-element.70), channel_id=1, source_target_pairs={{0,1},{1,2},{2,3},{3,4},{4,5},{5,6},{6,7},{7,8},{8,9},{9,10},{10,1... | collective-permute-start | bytes 46088 | tf_op jit(solution)/shard_map/ppermute | solution.py:21
  33.6 1.6 slice_bitcast_fusion
  37.2 1.8 %reduce_sum.14 = f32[2,2,4,16,48,4]{3,2,5,4,1,0:T(4,128)} reshape(f32[2,2,64,192]{2,3,1,0:T(8,128)S(1)} %copy.28) | data formatting | bytes 393216 | tf_op jit(solution)/shard_map/reduce_sum | solution.py:75
  39.0 1.8 reduce_sum.18
  40.8 1.9 %maximum_convert_fusion.1 = f32[2,2,10,66,192]{4,3,2,1,0:T(8,128)S(1)} fusion(bf16[2,2,10,1,192]{4,3,2,1,0:T(2,128)(2,1)} %collective-permute-done.8, bf16[2,2,1,64,192]{4,3,2,1,0:T(8,128)(2,1)} %copy-done.13, bf16[2,2,8,64,192]{4,3,2,1,0:T(8,128)(2,1)} %copy-done.4, bf16[2,2,1,64,192]{4,3,2,1,0:T(8,128)(2,1)} %copy-done.12, ...), kind=kLoop, calls=%fused_computation.35 | loop fusion | flops 5068800 | bytes 3041280 | tf_op jit(solution)/shard_map/convert_element_type | solution.py:71
  46.0 1.3 collective-permute-start.10
  47.3 3.0 %collective-permute-start.9 = (bf16[2,2,1,64,192]{4,3,2,1,0:T(8,128)(2,1)S(1)}, bf16[2,2,1,64,192]{4,3,2,1,0:T(8,128)(2,1)S(1)}, u32[]{:S(2)}, u32[]{:S(2)}) collective-permute-start(bf16[2,2,1,64,192]{4,3,2,1,0:T(8,128)(2,1)S(1)} %get-tuple-element.74), channel_id=1, source_target_pairs={{0,16},{1,17},{2,18},{3,19},{4,20},{5,21},{6,22},{7,23},{8,24},{9,... | collective-permute-start | bytes 294920 | tf_op jit(solution)/shard_map/ppermute | solution.py:21
  51.3 4.6 %collective-permute-start.11 = (bf16[2,2,10,1,192]{4,3,2,1,0:T(2,128)(2,1)S(1)}, bf16[2,2,10,1,192]{4,3,2,1,0:T(2,128)(2,1)S(1)}, u32[]{:S(2)}, u32[]{:S(2)}) collective-permute-start(bf16[2,2,10,1,192]{4,3,2,1,0:T(2,128)(2,1)S(1)} %get-tuple-element.68), channel_id=1, source_target_pairs={{0,1},{1,2},{2,3},{3,4},{4,5},{5,6},{6,7},{7,8},{8,9},{9,10},{10,1... | collective-permute-start | bytes 46088 | tf_op jit(solution)/shard_map/ppermute | solution.py:21
  55.9 1.5 collective-permute-start.12
  57.4 115.7 %while.10 = (s32[]{:T(128)}, f32[2,2,192]{2,1,0:T(2,128)S(1)}, f32[2,2,192]{2,1,0:T(2,128)S(1)}, bf16[192,3072]{1,0:T(8,128)(2,1)}, bf16[192,3072]{1,0:T(8,128)(2,1)}, /*index=5*/s32[]{:T(128)}) while((s32[]{:T(128)}, f32[2,2,192]{2,1,0:T(2,128)S(1)}, f32[2,2,192]{2,1,0:T(2,128)S(1)}, bf16[192,3072]{1,0:T(8,128)(2,1)}, ...), condition=%wide.region_3.4_spmd, body=%wide.region_2.3_spmd.sunk | while | flops 9441026 | bytes 2528365 | solution.py:97
  57.4 2.0 %collective-permute-start = (f32[2,2,192]{2,1,0:T(2,128)S(1)}, f32[2,2,192]{2,1,0:T(2,128)S(1)}, u32[]{:S(2)}, u32[]{:S(2)}) collective-permute-start(f32[2,2,192]{2,1,0:T(2,128)S(1)} %get-tuple-element.126), channel_id=1, source_target_pairs={{0,16},{1,17},{2,18},{3,19},{4,20},{5,21},{6,22},{7,23},{8,24},{9,... | collective-permute-start | bytes 9224 | tf_op jit(solution)/shard_map/while/body/eval_jaxpr/ppermute | solution.py:32
  60.4 52.2 %all_gather.4 = bf16[2,2,3072]{1,0,2:T(2,128)(2,1)S(1)} all-gather(bf16[2,2,192]{1,0,2:T(2,128)(2,1)S(1)} %copy.36), channel_id=1, replica_groups=mesh['layer'=2,'row'=16] {'row'}, dimensions={2}, use_global_device_ids=true | all-gather | bytes 26112 | tf_op jit(solution)/shard_map/while/body/eval_jaxpr/all_gather | solution.py:95
  112.6 1.5 copy.37
  114.1 1.7 fusion.45
  115.8 1.7 fusion.46
  119.8 48.3 %all_gather.4 = bf16[2,2,3072]{1,0,2:T(2,128)(2,1)S(1)} all-gather(bf16[2,2,192]{1,0,2:T(2,128)(2,1)S(1)} %copy.36), channel_id=1, replica_groups=mesh['layer'=2,'row'=16] {'row'}, dimensions={2}, use_global_device_ids=true | all-gather | bytes 26112 | tf_op jit(solution)/shard_map/while/body/eval_jaxpr/all_gather | solution.py:95
  168.2 1.5 copy.37
  169.7 1.7 fusion.45
  171.4 1.7 fusion.46
  173.3 1.4 broadcast_in_dim.12
  174.8 2.1 %broadcast_in_dim.13 = f32[2,2,64,192]{2,3,1,0:T(8,128)S(1)} reshape(f32[2,2,4,16,48,4]{3,2,5,4,1,0:T(4,128)} %broadcast_in_dim.12) | data formatting | bytes 393216 | tf_op jit(solution)/shard_map/broadcast_in_dim | solution.py:99
  180.8 1.8 fusion.16
  (83 shorter events, 20.6 us)
Async XLA Ops:
  0.0 1.7 copy-start
  1.5 18.8 %copy-start.5 = (f32[8,64,192]{2,1,0:T(8,128)}, f32[8,64,192]{2,1,0:T(8,128)S(1)}, u32[]{:S(2)}) copy-start(f32[8,64,192]{2,1,0:T(8,128)S(1)} %get-tuple-element.80) | copy-start | bytes 1179652
  1.5 18.8 %copy-start.8 = (f32[8,64,192]{2,1,0:T(8,128)}, f32[8,64,192]{2,1,0:T(8,128)S(1)}, u32[]{:S(2)}) copy-start(f32[8,64,192]{2,1,0:T(8,128)S(1)} %get-tuple-element.83) | copy-start | bytes 1179652
  2.4 3.7 %collective-permute-start.1 = (bf16[2,2,1,64,192]{4,3,2,1,0:T(8,128)(2,1)S(1)}, bf16[2,2,1,64,192]{4,3,2,1,0:T(8,128)(2,1)S(1)}, u32[]{:S(2)}, u32[]{:S(2)}) collective-permute-start(bf16[2,2,1,64,192]{4,3,2,1,0:T(8,128)(2,1)S(1)} %get-tuple-element.78), channel_id=1, source_target_pairs={{0,16},{1,17},{2,18},{3,19},{4,20},{5,21},{6,22},{7,23},{8,24},{9,... | collective-permute-start | bytes 294920 | tf_op jit(solution)/shard_map/ppermute | solution.py:21
  4.8 3.2 %collective-permute-start.2 = (bf16[2,2,1,64,192]{4,3,2,1,0:T(8,128)(2,1)S(1)}, bf16[2,2,1,64,192]{4,3,2,1,0:T(8,128)(2,1)S(1)}, u32[]{:S(2)}, u32[]{:S(2)}) collective-permute-start(bf16[2,2,1,64,192]{4,3,2,1,0:T(8,128)(2,1)S(1)} %get-tuple-element.79), channel_id=1, source_target_pairs={{16,0},{17,1},{18,2},{19,3},{20,4},{21,5},{22,6},{23,7},{24,8},{25... | collective-permute-start | bytes 294920 | tf_op jit(solution)/shard_map/ppermute | solution.py:24
  8.1 5.9 %collective-permute-start.3 = (bf16[2,2,10,1,192]{4,3,2,1,0:T(2,128)(2,1)S(1)}, bf16[2,2,10,1,192]{4,3,2,1,0:T(2,128)(2,1)S(1)}, u32[]{:S(2)}, u32[]{:S(2)}) collective-permute-start(bf16[2,2,10,1,192]{4,3,2,1,0:T(2,128)(2,1)S(1)} %get-tuple-element.72), channel_id=1, source_target_pairs={{0,1},{1,2},{2,3},{3,4},{4,5},{5,6},{6,7},{7,8},{8,9},{9,10},{10,1... | collective-permute-start | bytes 46088 | tf_op jit(solution)/shard_map/ppermute | solution.py:21
  12.3 5.9 %collective-permute-start.4 = (bf16[2,2,10,1,192]{4,3,2,1,0:T(2,128)(2,1)S(1)}, bf16[2,2,10,1,192]{4,3,2,1,0:T(2,128)(2,1)S(1)}, u32[]{:S(2)}, u32[]{:S(2)}) collective-permute-start(bf16[2,2,10,1,192]{4,3,2,1,0:T(2,128)(2,1)S(1)} %get-tuple-element.73), channel_id=1, source_target_pairs={{1,0},{2,1},{3,2},{4,3},{5,4},{6,5},{7,6},{8,7},{9,8},{10,9},{11,1... | collective-permute-start | bytes 46088 | tf_op jit(solution)/shard_map/ppermute | solution.py:24
  21.5 12.1 %copy-start.11 = (bf16[2,1,192,3072]{3,2,1,0:T(8,128)(2,1)S(1)}, bf16[2,1,192,3072]{3,2,1,0:T(8,128)(2,1)}, u32[]{:S(2)}) copy-start(bf16[2,1,192,3072]{3,2,1,0:T(8,128)(2,1)} %param.7) | copy-start | bytes 7077892
  21.9 4.7 %copy-start.4 = (bf16[2,2,8,64,192]{4,3,2,1,0:T(8,128)(2,1)}, bf16[2,2,8,64,192]{4,3,2,1,0:T(8,128)(2,1)S(1)}, u32[]{:S(2)}) copy-start(bf16[2,2,8,64,192]{4,3,2,1,0:T(8,128)(2,1)S(1)} %fusion.12) | copy-start | bytes 2359300
  22.0 2.7 %collective-permute-start.5 = (bf16[2,2,1,64,192]{4,3,2,1,0:T(8,128)(2,1)S(1)}, bf16[2,2,1,64,192]{4,3,2,1,0:T(8,128)(2,1)S(1)}, u32[]{:S(2)}, u32[]{:S(2)}) collective-permute-start(bf16[2,2,1,64,192]{4,3,2,1,0:T(8,128)(2,1)S(1)} %get-tuple-element.76), channel_id=1, source_target_pairs={{0,16},{1,17},{2,18},{3,19},{4,20},{5,21},{6,22},{7,23},{8,24},{9,... | collective-permute-start | bytes 294920 | tf_op jit(solution)/shard_map/ppermute | solution.py:21
  23.4 3.2 %collective-permute-start.6 = (bf16[2,2,1,64,192]{4,3,2,1,0:T(8,128)(2,1)S(1)}, bf16[2,2,1,64,192]{4,3,2,1,0:T(8,128)(2,1)S(1)}, u32[]{:S(2)}, u32[]{:S(2)}) collective-permute-start(bf16[2,2,1,64,192]{4,3,2,1,0:T(8,128)(2,1)S(1)} %get-tuple-element.77), channel_id=1, source_target_pairs={{16,0},{17,1},{18,2},{19,3},{20,4},{21,5},{22,6},{23,7},{24,8},{25... | collective-permute-start | bytes 294920 | tf_op jit(solution)/shard_map/ppermute | solution.py:24
  24.7 2.6 %copy-start.12 = (bf16[2,2,1,64,192]{4,3,2,1,0:T(8,128)(2,1)}, bf16[2,2,1,64,192]{4,3,2,1,0:T(8,128)(2,1)S(1)}, u32[]{:S(2)}) copy-start(bf16[2,2,1,64,192]{4,3,2,1,0:T(8,128)(2,1)S(1)} %collective-permute-done.5) | copy-start | bytes 294916
  26.7 0.7 copy-start.13
  27.4 13.4 %collective-permute-start.7 = (bf16[2,2,10,1,192]{4,3,2,1,0:T(2,128)(2,1)}, bf16[2,2,10,1,192]{4,3,2,1,0:T(2,128)(2,1)}, u32[]{:S(2)}, u32[]{:S(2)}) collective-permute-start(bf16[2,2,10,1,192]{4,3,2,1,0:T(2,128)(2,1)} %get-tuple-element.70), channel_id=1, source_target_pairs={{0,1},{1,2},{2,3},{3,4},{4,5},{5,6},{6,7},{7,8},{8,9},{9,10},{10,1... | collective-permute-start | bytes 46088 | tf_op jit(solution)/shard_map/ppermute | solution.py:21
  32.3 8.6 %collective-permute-start.8 = (bf16[2,2,10,1,192]{4,3,2,1,0:T(2,128)(2,1)}, bf16[2,2,10,1,192]{4,3,2,1,0:T(2,128)(2,1)}, u32[]{:S(2)}, u32[]{:S(2)}) collective-permute-start(bf16[2,2,10,1,192]{4,3,2,1,0:T(2,128)(2,1)} %get-tuple-element.71), channel_id=1, source_target_pairs={{1,0},{2,1},{3,2},{4,3},{5,4},{6,5},{7,6},{8,7},{9,8},{10,9},{11,1... | collective-permute-start | bytes 46088 | tf_op jit(solution)/shard_map/ppermute | solution.py:24
  43.0 1.2 copy-start.6
  43.0 1.2 copy-start.9
  45.9 11.5 %copy-start.2 = (bf16[2,2,8,64,192]{4,3,2,1,0:T(8,128)(2,1)}, bf16[2,2,8,64,192]{4,3,2,1,0:T(8,128)(2,1)S(1)}, u32[]{:S(2)}) copy-start(bf16[2,2,8,64,192]{4,3,2,1,0:T(8,128)(2,1)S(1)} %fusion.14) | copy-start | bytes 2359300
  46.0 4.6 %collective-permute-start.10 = (bf16[2,2,1,64,192]{4,3,2,1,0:T(8,128)(2,1)S(1)}, bf16[2,2,1,64,192]{4,3,2,1,0:T(8,128)(2,1)S(1)}, u32[]{:S(2)}, u32[]{:S(2)}) collective-permute-start(bf16[2,2,1,64,192]{4,3,2,1,0:T(8,128)(2,1)S(1)} %get-tuple-element.75), channel_id=1, source_target_pairs={{16,0},{17,1},{18,2},{19,3},{20,4},{21,5},{22,6},{23,7},{24,8},{25... | collective-permute-start | bytes 294920 | tf_op jit(solution)/shard_map/ppermute | solution.py:24
  47.3 4.0 %collective-permute-start.9 = (bf16[2,2,1,64,192]{4,3,2,1,0:T(8,128)(2,1)S(1)}, bf16[2,2,1,64,192]{4,3,2,1,0:T(8,128)(2,1)S(1)}, u32[]{:S(2)}, u32[]{:S(2)}) collective-permute-start(bf16[2,2,1,64,192]{4,3,2,1,0:T(8,128)(2,1)S(1)} %get-tuple-element.74), channel_id=1, source_target_pairs={{0,16},{1,17},{2,18},{3,19},{4,20},{5,21},{6,22},{7,23},{8,24},{9,... | collective-permute-start | bytes 294920 | tf_op jit(solution)/shard_map/ppermute | solution.py:21
  51.3 125.7 %collective-permute-start.11 = (bf16[2,2,10,1,192]{4,3,2,1,0:T(2,128)(2,1)S(1)}, bf16[2,2,10,1,192]{4,3,2,1,0:T(2,128)(2,1)S(1)}, u32[]{:S(2)}, u32[]{:S(2)}) collective-permute-start(bf16[2,2,10,1,192]{4,3,2,1,0:T(2,128)(2,1)S(1)} %get-tuple-element.68), channel_id=1, source_target_pairs={{0,1},{1,2},{2,3},{3,4},{4,5},{5,6},{6,7},{7,8},{8,9},{9,10},{10,1... | collective-permute-start | bytes 46088 | tf_op jit(solution)/shard_map/ppermute | solution.py:21
  55.9 121.1 %collective-permute-start.12 = (bf16[2,2,10,1,192]{4,3,2,1,0:T(2,128)(2,1)S(1)}, bf16[2,2,10,1,192]{4,3,2,1,0:T(2,128)(2,1)S(1)}, u32[]{:S(2)}, u32[]{:S(2)}) collective-permute-start(bf16[2,2,10,1,192]{4,3,2,1,0:T(2,128)(2,1)S(1)} %get-tuple-element.69), channel_id=1, source_target_pairs={{1,0},{2,1},{3,2},{4,3},{5,4},{6,5},{7,6},{8,7},{9,8},{10,9},{11,1... | collective-permute-start | bytes 46088 | tf_op jit(solution)/shard_map/ppermute | solution.py:24
  57.4 2.8 %collective-permute-start = (f32[2,2,192]{2,1,0:T(2,128)S(1)}, f32[2,2,192]{2,1,0:T(2,128)S(1)}, u32[]{:S(2)}, u32[]{:S(2)}) collective-permute-start(f32[2,2,192]{2,1,0:T(2,128)S(1)} %get-tuple-element.126), channel_id=1, source_target_pairs={{0,16},{1,17},{2,18},{3,19},{4,20},{5,21},{6,22},{7,23},{8,24},{9,... | collective-permute-start | bytes 9224 | tf_op jit(solution)/shard_map/while/body/eval_jaxpr/ppermute | solution.py:32
  117.6 2.1 %collective-permute-start = (f32[2,2,192]{2,1,0:T(2,128)S(1)}, f32[2,2,192]{2,1,0:T(2,128)S(1)}, u32[]{:S(2)}, u32[]{:S(2)}) collective-permute-start(f32[2,2,192]{2,1,0:T(2,128)S(1)} %get-tuple-element.126), channel_id=1, source_target_pairs={{0,16},{1,17},{2,18},{3,19},{4,20},{5,21},{6,22},{7,23},{8,24},{9,... | collective-permute-start | bytes 9224 | tf_op jit(solution)/shard_map/while/body/eval_jaxpr/ppermute | solution.py:32
  173.3 3.7 %copy-start.3 = (bf16[2,2,8,64,192]{4,3,2,1,0:T(8,128)(2,1)S(1)}, bf16[2,2,8,64,192]{4,3,2,1,0:T(8,128)(2,1)}, u32[]{:S(2)}) copy-start(bf16[2,2,8,64,192]{4,3,2,1,0:T(8,128)(2,1)} %copy-done.2) | copy-start | bytes 2359300
  177.9 1.6 copy-start.1
  177.9 1.7 copy-start.7
  177.9 1.8 copy-start.10
where the time goes:
time: 183 us
  blocking collectives  101 us (55%)
  starting transfers between devices  31.7 us (17%)
  other arithmetic  18.3 us (10%)
  local copies, waits for them, and re-layouts  13.7 us (7%)
  waiting for transfers between devices  10.8 us (6%)
  matrix products  6.82 us (4%)
    all_gather x2, blocking collectives, advance_all(): return fold_into(lax.all_gather(vector, 'row', axis=2, tiled=True))  101 us
    ppermute x6, starting transfers between devices, extended_2(): lax.ppermute(lax.slice_in_dim(block, block.shape[dim] - width, None, axis...  20.5 us
    ppermute x6, waiting for transfers between devices, extended_2(): lax.ppermute(lax.slice_in_dim(block, 0, width, axis=dim), axis, backward)  8.11 us
    ppermute x6, starting transfers between devices, extended_2(): lax.ppermute(lax.slice_in_dim(block, 0, width, axis=dim), axis, backward)  7.92 us
    broadcast_in_dim x5, local copies, waits for them, and re-layouts, on_device(): jnp.broadcast_to(lifted, (shot_count, 2, slab_depth, height // QY, QY, ac...  3.87 us
  transfers between devices with their start and end apart: 14, of which 7 were waited for; matrix products, arithmetic and copies ran while one was open for 12% of the time, Pallas kernels for 0%

commit v1 on v0

v1 whole, which is shorter than its diff:
```python
import functools

import jax
import jax.numpy as jnp
from jax import lax
from jax.experimental import pallas as pl
from jax.experimental.pallas import tpu as pltpu
from jax.sharding import PartitionSpec as P

QY = 16
PX = 4
SWEEPS = 4

damping = 0.8
absorb = 0.5
coupling = 0.45

LANES = 128
SUB = 8
TOP = 8
MESH = pl.DeviceIdType.MESH
f32 = jnp.float32
bf16 = jnp.bfloat16


def split_rows(value):
    upper = value.astype(bf16).astype(f32)
    return jnp.concatenate([upper, value - upper], axis=0).astype(bf16)


def kernel(n_layer, n_row, res_hbm, wav_hbm, inv_hbm, out_hbm, lift_ref,
           res, wav, mat, place, recip, smooth, final, pool, gath, cgath, piece_buf, coarse_buf,
           ysend, yrecv, load_sem, gs_sem, gr_sem, cs_sem, cr_sem, zs_sem, zr_sem, ys_sem, yr_sem, out_sem):
    layer = lax.axis_index("layer")
    row = lax.axis_index("row")
    fields, depth, height, width = res.shape
    shots = fields // 2
    chunks = smooth.shape[3]
    wide = chunks * LANES
    tiles = height // SUB
    yblocks = height // QY
    xblocks = width // PX
    piece = yblocks * xblocks
    tail = width - (chunks - 1) * LANES

    load_res = pltpu.make_async_copy(res_hbm, res, load_sem.at[0])
    load_wav = pltpu.make_async_copy(wav_hbm, wav, load_sem.at[1])
    load_mat = pltpu.make_async_copy(inv_hbm, mat, load_sem.at[2])
    load_res.start()
    load_wav.start()
    load_mat.start()

    barrier = pltpu.get_barrier_semaphore()

    @pl.loop(1, n_row)
    def _(step):
        pl.semaphore_signal(barrier, inc=1, device_id=(layer, lax.rem(row + step, n_row)), device_id_type=MESH)

    @pl.when(layer < n_layer - 1)
    def _():
        @pl.loop(0, n_row)
        def _(target):
            pl.semaphore_signal(barrier, inc=1, device_id=(layer + 1, target), device_id_type=MESH)

    @pl.when(layer > 0)
    def _():
        @pl.loop(0, n_row)
        def _(target):
            pl.semaphore_signal(barrier, inc=1, device_id=(layer - 1, target), device_id_type=MESH)

    across = lax.broadcasted_iota(jnp.int32, (wide, wide), 0)
    cell = lax.broadcasted_iota(jnp.int32, (wide, wide), 1)
    for yc in range(yblocks):
        offset = across - PX * (cell - yc * xblocks)
        place[yc] = jnp.where((offset >= 0) & (offset < PX), 1.0, 0.0).astype(bf16)

    def widened(value):
        if value.shape[1] == LANES:
            return value
        return jnp.concatenate([value, jnp.zeros((value.shape[0], LANES - value.shape[1]), value.dtype)], axis=1)

    def part(ref, index, first, chunk):
        stop = min(width, (chunk + 1) * LANES)
        return widened(ref[(*index, pl.ds(first, SUB), pl.ds(chunk * LANES, stop - chunk * LANES))])

    load_res.wait()

    @pl.loop(0, yblocks)
    def _(yc):
        first = pl.multiple_of(yc * QY, QY)
        for field in range(fields):
            for chunk in range(chunks):
                stop = min(width, (chunk + 1) * LANES)
                total = None
                for z in range(depth):
                    for y in range(QY // SUB):
                        item = res[field, z, pl.ds(first + y * SUB, SUB), pl.ds(chunk * LANES, stop - chunk * LANES)]
                        total = item if total is None else total + item
                pool[yc, pl.ds(field, 1), pl.ds(chunk * LANES, LANES)] = widened(jnp.sum(total, axis=0, keepdims=True))

    summed = None
    for yc in range(yblocks):
        product = jnp.dot(split_rows(pool[yc]), place[yc], preferred_element_type=f32)
        summed = product if summed is None else summed + product
    own = (summed[:fields] + summed[fields:]) * (1.0 / (depth * QY * PX))
    shift = lax.rem(row * piece, LANES)
    own = pltpu.roll(own, shift, 1)
    piece_buf[...] = own
    gath[row] = own

    count = (n_row - 1) + jnp.where(layer < n_layer - 1, n_row, 0) + jnp.where(layer > 0, n_row, 0)
    pl.semaphore_wait(barrier, count)

    def gather_copy(target, slot_send, slot_recv):
        return pltpu.make_async_remote_copy(
            src_ref=piece_buf, dst_ref=gath.at[slot_recv], send_sem=gs_sem.at[slot_send], recv_sem=gr_sem.at[slot_recv],
            device_id=(layer, target), device_id_type=MESH)

    @pl.loop(1, n_row)
    def _(step):
        target = lax.rem(row + step, n_row)
        gather_copy(target, target, row).start()

    load_wav.wait()

    @pl.loop(0, depth)
    def _(z):
        for tile in range(tiles):
            rows = pl.ds(tile * SUB, SUB)
            for chunk in range(chunks):
                wave = part(wav, (z,), tile * SUB, chunk)
                real = 6.0 - wave
                imag = absorb * wave
                scale = damping / (real * real + imag * imag)
                g_re = real * scale
                g_im = imag * scale
                if chunk == chunks - 1 and tail < LANES:
                    inside = lax.broadcasted_iota(jnp.int32, (SUB, LANES), 1) < tail
                    g_re = jnp.where(inside, g_re, 0.0)
                    g_im = jnp.where(inside, g_im, 0.0)
                recip[0, z, chunk, rows, :] = g_re
                recip[1, z, chunk, rows, :] = g_im
                for shot in range(shots):
                    r_re = part(res, (2 * shot, z), tile * SUB, chunk)
                    r_im = part(res, (2 * shot + 1, z), tile * SUB, chunk)
                    inner = pl.ds(TOP + tile * SUB, SUB)
                    smooth[0, 2 * shot, z + 1, chunk, inner, :] = g_re * r_re - g_im * r_im
                    smooth[0, 2 * shot + 1, z + 1, chunk, inner, :] = g_re * r_im + g_im * r_re

    inner_rows = pl.ds(TOP, height)

    def z_copy(k, way):
        source, target = ((depth, 0), (1, depth + 1))[way]
        return pltpu.make_async_remote_copy(
            src_ref=smooth.at[k, :, source, :, inner_rows, :], dst_ref=smooth.at[k, :, target, :, inner_rows, :],
            send_sem=zs_sem.at[k, way], recv_sem=zr_sem.at[k, way],
            device_id=(layer + (1, -1)[way], row), device_id_type=MESH)

    def y_copy(k, way):
        return pltpu.make_async_remote_copy(
            src_ref=ysend.at[k, way], dst_ref=yrecv.at[k, way],
            send_sem=ys_sem.at[k, way], recv_sem=yr_sem.at[k, way],
            device_id=(layer, row + (1, -1)[way]), device_id_type=MESH)

    has_next = {"z": layer < n_layer - 1, "y": row < n_row - 1}
    has_last = {"z": layer > 0, "y": row > 0}

    def send_halo(k):
        for way, able in ((0, has_next["z"]), (1, has_last["z"])):
            @pl.when(able)
            def _():
                z_copy(k, way).start()

        @pl.loop(0, fields)
        def _(field):
            for z in range(depth):
                for chunk in range(chunks):
                    ysend[k, 0, field, chunk, pl.ds(z, 1), :] = smooth[k, field, z + 1, chunk, pl.ds(TOP + height - 1, 1), :]
                    ysend[k, 1, field, chunk, pl.ds(z, 1), :] = smooth[k, field, z + 1, chunk, pl.ds(TOP, 1), :]

        for way, able in ((0, has_next["y"]), (1, has_last["y"])):
            @pl.when(able)
            def _():
                y_copy(k, way).start()

    for way, able in ((0, has_last["z"]), (1, has_next["z"])):
        @pl.when(jnp.logical_not(able))
        def _():
            for k in range(SWEEPS - 1):
                @pl.loop(0, fields)
                def _(field):
                    for chunk in range(chunks):
                        smooth[k, field, (0, depth + 1)[way], chunk, inner_rows, :] = jnp.zeros((height, LANES), f32)
    for way, able in ((0, has_last["y"]), (1, has_next["y"])):
        @pl.when(jnp.logical_not(able))
        def _():
            for k in range(SWEEPS - 1):
                yrecv[k, way] = jnp.zeros(yrecv.shape[2:], f32)

    def take_halo(k):
        for way, z_able, y_able in ((0, has_last["z"], has_last["y"]), (1, has_next["z"], has_next["y"])):
            @pl.when(z_able)
            def _():
                z_copy(k, way).wait_recv()

            @pl.when(y_able)
            def _():
                y_copy(k, way).wait_recv()

        @pl.loop(0, fields)
        def _(field):
            for z in range(depth):
                for chunk in range(chunks):
                    smooth[k, field, z + 1, chunk, pl.ds(TOP - 1, 1), :] = yrecv[k, 0, field, chunk, pl.ds(z, 1), :]
                    smooth[k, field, z + 1, chunk, pl.ds(TOP + height, 1), :] = yrecv[k, 1, field, chunk, pl.ds(z, 1), :]

    def sweep(k):
        last = k == SWEEPS - 2
        lane = lax.broadcasted_iota(jnp.int32, (SUB, LANES), 1)
        first_lane, last_lane = lane == 0, lane == LANES - 1

        @pl.loop(0, depth * shots)
        def _(index):
            z = lax.div(index, shots)
            shot = lax.rem(index, shots)
            for tile in range(tiles):
                y0 = TOP + tile * SUB
                beside, centre = [], []
                for p in range(2):
                    field = 2 * shot + p
                    mid = [smooth[k, field, z + 1, c, pl.ds(y0, SUB), :] for c in range(chunks)]
                    up = [pltpu.roll(m, 1, 1) for m in mid]
                    down = [pltpu.roll(m, LANES - 1, 1) for m in mid]
                    sums = []
                    for c in range(chunks):
                        total = (smooth[k, field, z, c, pl.ds(y0, SUB), :] + smooth[k, field, z + 2, c, pl.ds(y0, SUB), :]) + (
                            smooth[k, field, z + 1, c, pl.ds(y0 - 1, SUB), :] + smooth[k, field, z + 1, c, pl.ds(y0 + 1, SUB), :])
                        before = jnp.where(first_lane, up[c - 1], up[c])
                        after = jnp.where(last_lane, down[c + 1], down[c]) if c < chunks - 1 else down[c]
                        sums.append(total + (before + after))
                    beside.append(sums)
                    centre.append(mid)
                for c in range(chunks):
                    g_re = recip[0, z, c, pl.ds(tile * SUB, SUB), :]
                    g_im = recip[1, z, c, pl.ds(tile * SUB, SUB), :]
                    moved = (g_re * beside[0][c] - g_im * beside[1][c], g_re * beside[1][c] + g_im * beside[0][c])
                    for p in range(2):
                        field = 2 * shot + p
                        value = (1.0 - damping) * centre[p][c] + moved[p]
                        value = value + (centre[p][c] if k == 0 else smooth[0, field, z + 1, c, pl.ds(y0, SUB), :])
                        if last:
                            stop = min(width, (c + 1) * LANES) - c * LANES
                            final[field, z, pl.ds(tile * SUB, SUB), pl.ds(c * LANES, stop)] = value[:, :stop]
                        else:
                            smooth[k + 1, field, z + 1, c, pl.ds(y0, SUB), :] = value

    def coarse_copy(target, slot_send, slot_recv):
        return pltpu.make_async_remote_copy(
            src_ref=coarse_buf, dst_ref=cgath.at[slot_recv], send_sem=cs_sem.at[slot_send], recv_sem=cr_sem.at[slot_recv],
            device_id=(layer + 1, target), device_id_type=MESH)

    def wait_gather():
        @pl.loop(1, n_row)
        def _(step):
            source = lax.rem(row + step, n_row)
            gather_copy(source, source, source).wait_recv()

    def solve(fed):
        parts = [None] * (mat.shape[2] // LANES)
        for source in range(n_row):
            value = gath[source]
            if fed:
                value = value + coupling * cgath[source]
            start = source * piece // LANES
            for c in range(chunks):
                if start + c < len(parts):
                    item = value[:, c * LANES:(c + 1) * LANES]
                    parts[start + c] = item if parts[start + c] is None else parts[start + c] + item
        vector = jnp.concatenate(parts, axis=1).astype(bf16)
        dims = (((1,), (1,)), ((), ()))
        by_re = lax.dot_general(vector, mat[0], dims, preferred_element_type=f32)
        by_im = lax.dot_general(vector, mat[1], dims, preferred_element_type=f32)
        rows = []
        for shot in range(shots):
            a, b = 2 * shot, 2 * shot + 1
            rows.append(by_re[a:a + 1] - by_im[b:b + 1])
            rows.append(by_re[b:b + 1] + by_im[a:a + 1])
        coarse = jnp.concatenate(rows, axis=0)
        coarse = jnp.concatenate([coarse, jnp.zeros((fields, wide - piece), f32)], axis=1)
        coarse_buf[...] = pltpu.roll(coarse, shift, 1)

        @pl.when(layer < n_layer - 1)
        def _():
            @pl.loop(0, n_row)
            def _(step):
                target = lax.rem(row + step, n_row)
                coarse_copy(target, target, row).start()

        halves = split_rows(coarse)
        for yc in range(yblocks):
            raised = lax.dot_general(halves, place[yc], dims, preferred_element_type=f32)
            raised = raised[:fields] + raised[fields:]
            for field in range(fields):
                lift_ref[field, pl.ds(yc, 1), :] = raised[field:field + 1]

    send_halo(0)

    @pl.when(layer == 0)
    def _():
        load_mat.wait()
        wait_gather()
        solve(False)

    for k in range(SWEEPS - 1):
        take_halo(k)
        sweep(k)
        if k < SWEEPS - 2:
            send_halo(k + 1)

    store = pltpu.make_async_copy(final, out_hbm, out_sem)
    store.start()

    @pl.when(layer > 0)
    def _():
        load_mat.wait()
        wait_gather()

        @pl.loop(0, n_row)
        def _(step):
            source = lax.rem(row + step, n_row)
            coarse_copy(source, source, source).wait_recv()

        solve(True)

    store.wait()

    @pl.loop(1, n_row)
    def _(step):
        target = lax.rem(row + step, n_row)
        gather_copy(target, target, target).wait_send()

    @pl.when(layer < n_layer - 1)
    def _():
        @pl.loop(0, n_row)
        def _(target):
            coarse_copy(target, target, target).wait_send()

    for k in range(SWEEPS - 1):
        for way, z_able, y_able in ((0, has_next["z"], has_next["y"]), (1, has_last["z"], has_last["y"])):
            @pl.when(z_able)
            def _():
                z_copy(k, way).wait_send()

            @pl.when(y_able)
            def _():
                y_copy(k, way).wait_send()


def on_device(residual, wavenumber, inverse):
    n_layer, n_row = lax.axis_size("layer"), lax.axis_size("row")
    shots, _, depth, height, width = residual.shape
    fields = 2 * shots
    chunks = pl.cdiv(width, LANES)
    wide = chunks * LANES
    yblocks = height // QY
    _, _, rows, order = inverse.shape
    sweeps = SWEEPS - 1
    dma = pltpu.SemaphoreType.DMA
    smoothed, lifted = pl.pallas_call(
        functools.partial(kernel, n_layer, n_row),
        out_shape=(jax.ShapeDtypeStruct((fields, depth, height, width), f32),
                   jax.ShapeDtypeStruct((fields, yblocks, wide), f32)),
        in_specs=[pl.BlockSpec(memory_space=pl.ANY)] * 3,
        out_specs=(pl.BlockSpec(memory_space=pl.ANY), pl.BlockSpec(memory_space=pltpu.VMEM)),
        scratch_shapes=[
            pltpu.VMEM((fields, depth, height, width), f32),
            pltpu.VMEM((depth, height, width), f32),
            pltpu.VMEM((2, rows, order), bf16),
            pltpu.VMEM((yblocks, wide, wide), bf16),
            pltpu.VMEM((2, depth, chunks, height, LANES), f32),
            pltpu.VMEM((sweeps, fields, depth + 2, chunks, height + 2 * TOP, LANES), f32),
            pltpu.VMEM((fields, depth, height, width), f32),
            pltpu.VMEM((yblocks, fields, wide), f32),
            pltpu.VMEM((n_row, fields, wide), f32),
            pltpu.VMEM((n_row, fields, wide), f32),
            pltpu.VMEM((fields, wide), f32),
            pltpu.VMEM((fields, wide), f32),
            pltpu.VMEM((sweeps, 2, fields, chunks, depth, LANES), f32),
            pltpu.VMEM((sweeps, 2, fields, chunks, depth, LANES), f32),
            dma((3,)), dma((n_row,)), dma((n_row,)), dma((n_row,)), dma((n_row,)),
            dma((sweeps, 2)), dma((sweeps, 2)), dma((sweeps, 2)), dma((sweeps, 2)), dma,
        ],
        compiler_params=pltpu.CompilerParams(
            collective_id=0, has_side_effects=True, vmem_limit_bytes=40 * 1024 * 1024),
    )(residual.reshape(fields, depth, height, width), wavenumber, inverse.reshape(2, rows, order))
    lifted = lifted[:, :, :width].reshape(shots, 2, 1, yblocks, 1, width)
    smoothed = smoothed.reshape(shots, 2, depth, yblocks, QY, width)
    return (smoothed + lifted).reshape(residual.shape)


def solution(mesh):
    return jax.shard_map(
        on_device,
        mesh=mesh,
        in_specs=(
            P(None, None, "layer", "row", None),
            P("layer", "row", None),
            P(None, "layer", "row", None),
        ),
        out_specs=P(None, None, "layer", "row", None),
        check_vma=False,
    )
```

time: 183 us -> 33.5 us (0.18)
  blocking collectives: 101 us -> 0 us
  starting transfers between devices: 31.7 us -> 0 us
  Pallas kernels: 0 us -> 27.3 us
  other arithmetic: 18.3 us -> 1.59 us
  waiting for transfers between devices: 10.8 us -> 0 us
  local copies, waits for them, and re-layouts: 13.7 us -> 4.32 us
  matrix products: 6.82 us -> 0 us
    all_gather x2 -> x0, blocking collectives: 101 us -> none  [advance_all(): return fold_into(lax.all_gather(vector, 'row', axis=2, tiled=True))]
    ppermute x14 -> x0, starting transfers between devices: 31.7 us -> none  [the longest x6 20.5 us: extended_2(): lax.ppermute(lax.slice_in_dim(block, block.shape[dim] - width, None, axis...]
    pallas_call x0 -> x1, Pallas kernels: none -> 27.3 us  [on_device(): pl.pallas_call(functools.partial(kernel, n_layer, n_row), out_shape=(jax....]
    ppermute x14 -> x0, waiting for transfers between devices: 10.8 us -> none  [the longest x6 8.11 us: extended_2(): lax.ppermute(lax.slice_in_dim(block, 0, width, axis=dim), axis, backward)]
    dot_general x4 -> x0, matrix products: 6.82 us -> none  [the longest x2 3.42 us: fold_into(): jnp.einsum('rc,ksc->ksr', matrix_re, shard_piece, preferred_element_type=...]
    sub x7 -> x0, other arithmetic: 4.61 us -> none  [the longest x3 2.83 us: relax(): update_re = reciprocal_re * remain_re - reciprocal_im * remain_im]
    add x7 -> x1, other arithmetic: 5.98 us -> 1.59 us  [on_device(): return (smoothed + lifted).reshape(residual.shape)]
    convert_element_type x8 -> x0, other arithmetic: 4.14 us -> none  [the longest x3 2.92 us: on_device(): extended_2(iterate.astype(jnp.bfloat16), (('layer', 2), ('row', 3)), 1)]
  transfers between devices with their start and end apart: 14 -> 0, of which waited for: 7 -> 0; matrix products, arithmetic and copies ran while one was open for 12% -> 0% of each run, Pallas kernels for 0% -> 0%
where the time goes in v1:
time: 33.5 us; the launch traced here: 33.3 us
  Pallas kernels  27.3 us (81%)
  local copies, waits for them, and re-layouts  4.32 us (13%)
  other arithmetic  1.59 us (5%)
    pallas_call x1, Pallas kernels, on_device(): pl.pallas_call(functools.partial(kernel, n_layer, n_row), out_shape=(jax....  27.3 us
    unnamed x6, local copies, waits for them, and re-layouts  4.3 us
    add x1, other arithmetic, on_device(): return (smoothed + lifted).reshape(residual.shape)  1.59 us

profile of v1, /device:TPU:0, one launch (start us, length us, event | category | flops | bytes accessed | tf_op | source)
XLA Modules:
  0.0 33.3 jit_solution(16557406434040006666)
XLA Ops:
  0.0 0.0 copy-start
  0.0 1.7 %copy-done = bf16[2,1,192,3072]{3,2,1,0:T(8,128)(2,1)S(1)} copy-done((bf16[2,1,192,3072]{3,2,1,0:T(8,128)(2,1)S(1)}, bf16[2,1,192,3072]{3,2,1,0:T(8,128)(2,1)}, u32[]{:S(2)}) %copy-start) | copy-done | bytes 2359320
  1.7 0.0 copy-start.1
  1.7 1.6 %copy-done.1 = f32[2,2,8,64,192]{4,3,2,1,0:T(8,128)S(1)} copy-done((f32[2,2,8,64,192]{4,3,2,1,0:T(8,128)S(1)}, f32[2,2,8,64,192]{4,3,2,1,0:T(8,128)}, u32[]{:S(2)}) %copy-start.1) | copy-done | bytes 1572888
  3.3 0.0 copy-start.2
  3.3 1.0 %copy-done.2 = f32[8,64,192]{2,1,0:T(8,128)S(1)} copy-done((f32[8,64,192]{2,1,0:T(8,128)S(1)}, f32[8,64,192]{2,1,0:T(8,128)}, u32[]{:S(2)}) %copy-start.2) | copy-done | bytes 393240
  4.3 27.3 %shard_map.37 = (f32[4,8,64,192]{3,2,1,0:T(8,128)S(1)}, f32[4,4,256]{2,1,0:T(4,128)S(1)}) custom-call(f32[4,8,64,192]{3,2,1,0:T(8,128)S(1)} %bitcast.7, f32[8,64,192]{2,1,0:T(8,128)S(1)} %copy-done.2, bf16[2,192,3072]{2,1,0:T(8,128)(2,1)S(1)} %bitcast.6), custom_call_target="tpu_custom_call" | custom-call | tf_op jit(solution)/shard_map/pallas_call | solution.py:369
  31.7 1.6 %broadcast_add_fusion = f32[2,2,8,64,192]{4,3,2,1,0:T(8,128)} fusion(f32[2,2,8,64,192]{4,3,2,1,0:T(8,128)S(1)} %bitcast.8, f32[2,2,64,192]{3,2,1,0:T(8,128)S(1)} %bitcast.10), kind=kLoop, calls=%fused_computation | loop fusion | flops 393216 | bytes 3342336 | tf_op jit(solution)/shard_map/add | solution.py:398
  (1 shorter events, 0.0 us)
Async XLA Ops:
  0.0 1.7 %copy-start = (bf16[2,1,192,3072]{3,2,1,0:T(8,128)(2,1)S(1)}, bf16[2,1,192,3072]{3,2,1,0:T(8,128)(2,1)}, u32[]{:S(2)}) copy-start(bf16[2,1,192,3072]{3,2,1,0:T(8,128)(2,1)} %param.5) | copy-start | bytes 7077892
  1.7 1.6 %copy-start.1 = (f32[2,2,8,64,192]{4,3,2,1,0:T(8,128)S(1)}, f32[2,2,8,64,192]{4,3,2,1,0:T(8,128)}, u32[]{:S(2)}) copy-start(f32[2,2,8,64,192]{4,3,2,1,0:T(8,128)} %param.3) | copy-start | bytes 4718596
  3.3 1.0 %copy-start.2 = (f32[8,64,192]{2,1,0:T(8,128)S(1)}, f32[8,64,192]{2,1,0:T(8,128)}, u32[]{:S(2)}) copy-start(f32[8,64,192]{2,1,0:T(8,128)} %wav_hbm.1) | copy-start | bytes 1179652

commit v2 on v1

--- a/solution.py
+++ b/solution.py
@@ -48,7 +48,6 @@
     load_mat = pltpu.make_async_copy(inv_hbm, mat, load_sem.at[2])
     load_res.start()
     load_wav.start()
-    load_mat.start()
 
     barrier = pltpu.get_barrier_semaphore()
 
@@ -83,7 +82,26 @@
         stop = min(width, (chunk + 1) * LANES)
         return widened(ref[(*index, pl.ds(first, SUB), pl.ds(chunk * LANES, stop - chunk * LANES))])
 
+    inner_rows = pl.ds(TOP, height)
+    has_next = {"z": layer < n_layer - 1, "y": row < n_row - 1}
+    has_last = {"z": layer > 0, "y": row > 0}
+
+    for way, able in ((0, has_last["z"]), (1, has_next["z"])):
+        @pl.when(jnp.logical_not(able))
+        def _():
+            for k in range(SWEEPS - 1):
+                @pl.loop(0, fields)
+                def _(field):
+                    for chunk in range(chunks):
+                        smooth[k, field, (0, depth + 1)[way], chunk, inner_rows, :] = jnp.zeros((height, LANES), f32)
+    for way, able in ((0, has_last["y"]), (1, has_next["y"])):
+        @pl.when(jnp.logical_not(able))
+        def _():
+            for k in range(SWEEPS - 1):
+                yrecv[k, way] = jnp.zeros(yrecv.shape[2:], f32)
+
     load_res.wait()
+    load_mat.start()
 
     @pl.loop(0, yblocks)
     def _(yc):
@@ -147,8 +165,6 @@
                     smooth[0, 2 * shot, z + 1, chunk, inner, :] = g_re * r_re - g_im * r_im
                     smooth[0, 2 * shot + 1, z + 1, chunk, inner, :] = g_re * r_im + g_im * r_re
 
-    inner_rows = pl.ds(TOP, height)
-
     def z_copy(k, way):
         source, target = ((depth, 0), (1, depth + 1))[way]
         return pltpu.make_async_remote_copy(
@@ -162,9 +178,6 @@
             send_sem=ys_sem.at[k, way], recv_sem=yr_sem.at[k, way],
             device_id=(layer, row + (1, -1)[way]), device_id_type=MESH)
 
-    has_next = {"z": layer < n_layer - 1, "y": row < n_row - 1}
-    has_last = {"z": layer > 0, "y": row > 0}
-
     def send_halo(k):
         for way, able in ((0, has_next["z"]), (1, has_last["z"])):
             @pl.when(able)
@@ -183,20 +196,6 @@
             def _():
                 y_copy(k, way).start()
 
-    for way, able in ((0, has_last["z"]), (1, has_next["z"])):
-        @pl.when(jnp.logical_not(able))
-        def _():
-            for k in range(SWEEPS - 1):
-                @pl.loop(0, fields)
-                def _(field):
-                    for chunk in range(chunks):
-                        smooth[k, field, (0, depth + 1)[way], chunk, inner_rows, :] = jnp.zeros((height, LANES), f32)
-    for way, able in ((0, has_last["y"]), (1, has_next["y"])):
-        @pl.when(jnp.logical_not(able))
-        def _():
-            for k in range(SWEEPS - 1):
-                yrecv[k, way] = jnp.zeros(yrecv.shape[2:], f32)
-
     def take_halo(k):
         for way, z_able, y_able in ((0, has_last["z"], has_last["y"]), (1, has_next["z"], has_next["y"])):
             @pl.when(z_able)
@@ -214,45 +213,54 @@
                     smooth[k, field, z + 1, chunk, pl.ds(TOP - 1, 1), :] = yrecv[k, 0, field, chunk, pl.ds(z, 1), :]
                     smooth[k, field, z + 1, chunk, pl.ds(TOP + height, 1), :] = yrecv[k, 1, field, chunk, pl.ds(z, 1), :]
 
-    def sweep(k):
+    def relax(k, z, shot, which):
         last = k == SWEEPS - 2
         lane = lax.broadcasted_iota(jnp.int32, (SUB, LANES), 1)
         first_lane, last_lane = lane == 0, lane == LANES - 1
-
-        @pl.loop(0, depth * shots)
-        def _(index):
-            z = lax.div(index, shots)
-            shot = lax.rem(index, shots)
-            for tile in range(tiles):
-                y0 = TOP + tile * SUB
-                beside, centre = [], []
+        for tile in which:
+            y0 = TOP + tile * SUB
+            beside, centre = [], []
+            for p in range(2):
+                field = 2 * shot + p
+                mid = [smooth[k, field, z + 1, c, pl.ds(y0, SUB), :] for c in range(chunks)]
+                up = [pltpu.roll(m, 1, 1) for m in mid]
+                down = [pltpu.roll(m, LANES - 1, 1) for m in mid]
+                sums = []
+                for c in range(chunks):
+                    total = (smooth[k, field, z, c, pl.ds(y0, SUB), :] + smooth[k, field, z + 2, c, pl.ds(y0, SUB), :]) + (
+                        smooth[k, field, z + 1, c, pl.ds(y0 - 1, SUB), :] + smooth[k, field, z + 1, c, pl.ds(y0 + 1, SUB), :])
+                    before = jnp.where(first_lane, up[c - 1], up[c])
+                    after = jnp.where(last_lane, down[c + 1], down[c]) if c < chunks - 1 else down[c]
+                    sums.append(total + (before + after))
+                beside.append(sums)
+                centre.append(mid)
+            for c in range(chunks):
+                g_re = recip[0, z, c, pl.ds(tile * SUB, SUB), :]
+                g_im = recip[1, z, c, pl.ds(tile * SUB, SUB), :]
+                moved = (g_re * beside[0][c] - g_im * beside[1][c], g_re * beside[1][c] + g_im * beside[0][c])
                 for p in range(2):
                     field = 2 * shot + p
-                    mid = [smooth[k, field, z + 1, c, pl.ds(y0, SUB), :] for c in range(chunks)]
-                    up = [pltpu.roll(m, 1, 1) for m in mid]
-                    down = [pltpu.roll(m, LANES - 1, 1) for m in mid]
-                    sums = []
-                    for c in range(chunks):
-                        total = (smooth[k, field, z, c, pl.ds(y0, SUB), :] + smooth[k, field, z + 2, c, pl.ds(y0, SUB), :]) + (
-                            smooth[k, field, z + 1, c, pl.ds(y0 - 1, SUB), :] + smooth[k, field, z + 1, c, pl.ds(y0 + 1, SUB), :])
-                        before = jnp.where(first_lane, up[c - 1], up[c])
-                        after = jnp.where(last_lane, down[c + 1], down[c]) if c < chunks - 1 else down[c]
-                        sums.append(total + (before + after))
-                    beside.append(sums)
-                    centre.append(mid)
-                for c in range(chunks):
-                    g_re = recip[0, z, c, pl.ds(tile * SUB, SUB), :]
-                    g_im = recip[1, z, c, pl.ds(tile * SUB, SUB), :]
-                    moved = (g_re * beside[0][c] - g_im * beside[1][c], g_re * beside[1][c] + g_im * beside[0][c])
-                    for p in range(2):
-                        field = 2 * shot + p
-                        value = (1.0 - damping) * centre[p][c] + moved[p]
-                        value = value + (centre[p][c] if k == 0 else smooth[0, field, z + 1, c, pl.ds(y0, SUB), :])
-                        if last:
-                            stop = min(width, (c + 1) * LANES) - c * LANES
-                            final[field, z, pl.ds(tile * SUB, SUB), pl.ds(c * LANES, stop)] = value[:, :stop]
-                        else:
-                            smooth[k + 1, field, z + 1, c, pl.ds(y0, SUB), :] = value
+                    value = (1.0 - damping) * centre[p][c] + moved[p]
+                    value = value + (centre[p][c] if k == 0 else smooth[0, field, z + 1, c, pl.ds(y0, SUB), :])
+                    if last:
+                        stop = min(width, (c + 1) * LANES) - c * LANES
+                        final[field, z, pl.ds(tile * SUB, SUB), pl.ds(c * LANES, stop)] = value[:, :stop]
+                    else:
+                        smooth[k + 1, field, z + 1, c, pl.ds(y0, SUB), :] = value
+
+    def inside(k):
+        @pl.loop(0, (depth - 2) * shots)
+        def _(index):
+            relax(k, 1 + lax.div(index, shots), lax.rem(index, shots), range(1, tiles - 1))
+
+    def rim(k):
+        @pl.loop(0, 2 * shots)
+        def _(index):
+            relax(k, lax.div(index, shots) * (depth - 1), lax.rem(index, shots), range(tiles))
+
+        @pl.loop(0, (depth - 2) * shots)
+        def _(index):
+            relax(k, 1 + lax.div(index, shots), lax.rem(index, shots), (0, tiles - 1))
 
     def coarse_copy(target, slot_send, slot_recv):
         return pltpu.make_async_remote_copy(
@@ -304,18 +312,18 @@
                 lift_ref[field, pl.ds(yc, 1), :] = raised[field:field + 1]
 
     send_halo(0)
-
-    @pl.when(layer == 0)
-    def _():
-        load_mat.wait()
-        wait_gather()
-        solve(False)
-
     for k in range(SWEEPS - 1):
+        inside(k)
         take_halo(k)
-        sweep(k)
+        rim(k)
         if k < SWEEPS - 2:
             send_halo(k + 1)
+        if k == 0:
+            @pl.when(layer == 0)
+            def _():
+                load_mat.wait()
+                wait_gather()
+                solve(False)
 
     store = pltpu.make_async_copy(final, out_hbm, out_sem)
     store.start()
@@ -370,7 +378,7 @@
         functools.partial(kernel, n_layer, n_row),
         out_shape=(jax.ShapeDtypeStruct((fields, depth, height, width), f32),
                    jax.ShapeDtypeStruct((fields, yblocks, wide), f32)),
-        in_specs=[pl.BlockSpec(memory_space=pl.ANY)] * 3,
+        in_specs=[pl.BlockSpec(memory_space=pltpu.HBM)] * 3,
         out_specs=(pl.BlockSpec(memory_space=pl.ANY), pl.BlockSpec(memory_space=pltpu.VMEM)),
         scratch_shapes=[
             pltpu.VMEM((fields, depth, height, width), f32),
@@ -391,7 +399,7 @@
             dma((sweeps, 2)), dma((sweeps, 2)), dma((sweeps, 2)), dma((sweeps, 2)), dma,
         ],
         compiler_params=pltpu.CompilerParams(
-            collective_id=0, has_side_effects=True, vmem_limit_bytes=40 * 1024 * 1024),
+            collective_id=0, has_side_effects=True, vmem_limit_bytes=60 * 1024 * 1024),
     )(residual.reshape(fields, depth, height, width), wavenumber, inverse.reshape(2, rows, order))
     lifted = lifted[:, :, :width].reshape(shots, 2, 1, yblocks, 1, width)
     smoothed = smoothed.reshape(shots, 2, depth, yblocks, QY, width)

time: 33.5 us -> 30.2 us (0.901)
  local copies, waits for them, and re-layouts: 4.32 us -> 0.74 us
  other arithmetic: 1.59 us -> 3.18 us
  Pallas kernels: 27.3 us -> 26 us
    unnamed x6 -> x0, local copies, waits for them, and re-layouts: 4.3 us -> none
    add x1, other arithmetic: 1.59 us -> 3.18 us  [on_device(): return (smoothed + lifted).reshape(residual.shape)]
    pallas_call x1, Pallas kernels: 27.3 us -> 26 us  [on_device(): pl.pallas_call(functools.partial(kernel, n_layer, n_row), out_shape=(jax....]
    add x1, local copies, waits for them, and re-layouts: 0.02 us -> 0.74 us  [on_device(): return (smoothed + lifted).reshape(residual.shape)]
where the time goes in v2:
time: 30.2 us; the launch traced here: 29.9 us
  Pallas kernels  26 us (86%)
  other arithmetic  3.18 us (11%)
  local copies, waits for them, and re-layouts  0.74 us (2%)
    pallas_call x1, Pallas kernels, on_device(): pl.pallas_call(functools.partial(kernel, n_layer, n_row), out_shape=(jax....  26 us
    add x1, other arithmetic, on_device(): return (smoothed + lifted).reshape(residual.shape)  3.18 us
    add x1, local copies, waits for them, and re-layouts, on_device(): return (smoothed + lifted).reshape(residual.shape)  0.74 us

profile of v2, /device:TPU:0, one launch (start us, length us, event | category | flops | bytes accessed | tf_op | source)
XLA Modules:
  0.0 29.9 jit_solution(3762260445358903060)
XLA Ops:
  0.0 26.0 %shard_map.37 = (f32[4,8,64,192]{3,2,1,0:T(8,128)}, f32[4,4,256]{2,1,0:T(4,128)}) custom-call(f32[4,8,64,192]{3,2,1,0:T(8,128)} %bitcast.7, f32[8,64,192]{2,1,0:T(8,128)} %wav_hbm.1, bf16[2,192,3072]{2,1,0:T(8,128)(2,1)} %bitcast.6), custom_call_target="tpu_custom_call" | custom-call | tf_op jit(solution)/shard_map/pallas_call | solution.py:377
  26.0 0.7 %add.16 = f32[2,2,4,16,192]{4,3,2,1,0:T(8,128)S(1)} broadcast(f32[2,2,4,192]{3,2,1,0:T(4,128)} %bitcast.10), dimensions={0,1,2,4} | broadcast | bytes 208896 | tf_op jit(solution)/shard_map/add | solution.py:406
  26.8 3.2 %broadcast_add_fusion = f32[2,2,8,64,192]{4,3,2,1,0:T(8,128)} fusion(f32[2,2,8,64,192]{4,3,2,1,0:T(8,128)} %bitcast.8, f32[2,2,64,192]{3,2,1,0:T(8,128)S(1)} %bitcast.9), kind=kLoop, calls=%fused_computation | loop fusion | flops 393216 | bytes 3342336 | tf_op jit(solution)/shard_map/add | solution.py:406
